TPU v7x, 32 devices: a whole 2x2x4 slice. The times are simulated.
32 devices in a mesh: tm: 16 (over z, x, core), chan: 2 (over y).
Axes of the slice: x: 2, y: 2, z: 4, core: 2. Of those that a mesh axis runs over, the one named last changes fastest.
Arguments:
- signal: bfloat16 [8192, 256], P('tm', 'chan'), may hold values from -6 to 6
- skip_in: bfloat16 [8192, 256], P('tm', 'chan'), may hold values from -6 to 6
- tap_weight: bfloat16 [4, 2, 256, 512], replicated, may hold values from -0.25 to 0.25
- tap_bias: float32 [4, 512], replicated, may hold values from -3 to 3
- res_weight: bfloat16 [3, 256, 256], replicated, may hold values from -0.375 to 0.375
- skip_weight: bfloat16 [4, 256, 256], replicated, may hold values from -0.375 to 0.375
- head_w1: float32 [256, 256], replicated, may hold values from -0.375 to 0.375
- head_b1: float32 [256], replicated, may hold values from -3 to 3
- head_w2: float32 [256, 12], replicated, may hold values from -0.375 to 0.375
- head_second_bias: float32 [12], replicated, may hold values from -3 to 3
- event_bin: int32 [64], P('tm'), may hold values from 0 to 15
- observed: int32 [64], P('tm'), may hold values 0 or 1
- valid_len: int32 [1], replicated, may hold values from 7937 to 8192
Outputs:
- window_nll: float32 [64], P(('tm', 'chan'))
- grad_input: bfloat16 [8192, 256], P('tm', 'chan')
All inputs are finite; a program needn't handle non-finite values. No bound on the sum of `observed` on one device may be relied on, other than what follows from the above.
Results may differ from a plain program's by a relative error of at most 0.022.
Values may be sent and summed in bfloat16 or wider, within the bound.
A program may use at most 64 MiB of HBM per device.

v0:
```python
import jax
import jax.numpy as jnp
from jax import lax
from jax.sharding import PartitionSpec as P

WLEN = 128


def passed_along(block, axis, distance):
    devices = range(lax.axis_size(axis))
    route = [(i - distance, i) for i in devices if i - distance in devices]
    return lax.ppermute(block, axis, route)


def gate_values(preact, half_width):
    filters = jnp.tanh(preact[:, :half_width])
    gates = jax.nn.sigmoid(preact[:, half_width:])
    return (filters * gates).astype(jnp.bfloat16)


def gate_grads(preact, grad_gated, half_width):
    filters = jnp.tanh(preact[:, :half_width])
    gates = jax.nn.sigmoid(preact[:, half_width:])
    grad_filter = grad_gated * gates * (1.0 - filters * filters)
    gate_gradient = grad_gated * filters * gates * (1.0 - gates)
    return jnp.concatenate([grad_filter, gate_gradient], axis=1).astype(jnp.bfloat16)


def silu_slope(values):
    sig = jax.nn.sigmoid(values)
    return sig * (1.0 + values * (1.0 - sig))


def pool_windows(activity, keep_mask, window_len):
    row_count, width = activity.shape
    sums = (
        (activity * keep_mask[:, None])
        .reshape(row_count // window_len, window_len, width)
        .sum(axis=1)
    )
    counts = keep_mask.reshape(row_count // window_len, window_len).sum(axis=1)
    return sums / jnp.maximum(counts, 1.0)[:, None]


def window_loss(pooled, bins, flags, head_w1, head_b1, head_w2, head_second_bias):
    hidden = jax.nn.silu(jnp.dot(pooled, head_w1, precision=lax.Precision.HIGHEST) + head_b1)
    params = jnp.dot(hidden, head_w2, precision=lax.Precision.HIGHEST) + head_second_bias
    mixes = params.shape[1] // 3
    logits = 4.0 * jnp.tanh(params[:, :mixes])
    mixture_log_weight = logits - jnp.log(jnp.sum(jnp.exp(logits), axis=1, keepdims=True))
    log_scale = jnp.tanh(params[:, mixes : 2 * mixes])
    log_shape = 0.5 * jnp.tanh(params[:, 2 * mixes :])
    shape_value = jnp.exp(log_shape)
    log_time = jnp.log((bins.astype(jnp.float32) + 1.0) / 8.0)[:, None]
    ratio = log_time - log_scale
    power = jnp.exp(shape_value * ratio)
    log_density = log_shape - log_scale + (shape_value - 1.0) * ratio - power
    component = jnp.where(flags[:, None] == 1, log_density, -power)
    return -jnp.log(jnp.sum(jnp.exp(mixture_log_weight + component), axis=1))


def head_grads(pooled, bins, flags, head_w1, head_b1, head_w2, head_second_bias):

    def loss_of(values):
        return window_loss(values, bins, flags, head_w1, head_b1, head_w2, head_second_bias)

    nll_values, pullback = jax.vjp(loss_of, pooled)
    return (nll_values, pullback(jnp.ones_like(nll_values))[0])


def spread_rows(grad_pool, window_len):
    window_total_count, width = grad_pool.shape
    return jnp.broadcast_to(grad_pool[:, None, :], (window_total_count, window_len, width)).reshape(
        window_total_count * window_len, width
    )


def delay(values, shard_shift):
    return passed_along(values, "tm", shard_shift)


def advance(values, shard_shift):
    return passed_along(values, "tm", -shard_shift)


def own_columns(matrix, chan_at, chan_part, width):
    filter_cols = lax.dynamic_slice_in_dim(matrix, chan_at * chan_part, chan_part, 1)
    gate_cols = lax.dynamic_slice_in_dim(matrix, width + chan_at * chan_part, chan_part, 1)
    return jnp.concatenate([filter_cols, gate_cols], axis=1)


def local(
    signal,
    skip_in,
    tap_weight,
    tap_bias,
    res_weight,
    skip_weight,
    head_w1,
    head_b1,
    head_w2,
    head_second_bias,
    event_bin,
    observed,
    valid_len,
):
    chan_count = lax.axis_size("chan")
    chan_at = lax.axis_index("chan")
    shard_at = lax.axis_index("tm")
    shard_rows, chan_part = signal.shape
    width = chan_part * chan_count
    layers = tap_weight.shape[0]
    base_shift = lax.axis_size("tm") // 16
    windows_here = shard_rows // WLEN
    own_windows = windows_here // chan_count
    limit = valid_len[0]
    current = signal
    skip_sum = skip_in.astype(jnp.float32)
    preacts = []
    for layer_number in range(layers):
        tap_old = own_columns(tap_weight[layer_number, 0], chan_at, chan_part, width)
        tap_new = own_columns(tap_weight[layer_number, 1], chan_at, chan_part, width)
        bias_own = own_columns(tap_bias[layer_number][None, :], chan_at, chan_part, width)[0]
        whole = lax.all_gather(current, "chan", axis=1, tiled=True)
        delayed = delay(whole, base_shift * 2**layer_number)
        preact = jnp.dot(delayed, tap_old, preferred_element_type=jnp.float32)
        preact = preact + jnp.dot(whole, tap_new, preferred_element_type=jnp.float32) + bias_own
        gated = gate_values(preact, chan_part)
        preacts.append(preact)
        gated_all = lax.all_gather(gated, "chan", axis=1, tiled=True)
        if layer_number < layers - 1:
            res_cols = lax.dynamic_slice_in_dim(
                res_weight[layer_number], chan_at * chan_part, chan_part, 1
            )
            current = (
                current.astype(jnp.float32)
                + jnp.dot(gated_all, res_cols, preferred_element_type=jnp.float32)
            ).astype(jnp.bfloat16)
        skip_cols = lax.dynamic_slice_in_dim(
            skip_weight[layer_number], chan_at * chan_part, chan_part, 1
        )
        skip_sum = skip_sum + jnp.dot(gated_all, skip_cols, preferred_element_type=jnp.float32)
    positions = shard_at * shard_rows + jnp.arange(shard_rows, dtype=jnp.int32)
    keep_mask = (positions < limit).astype(jnp.float32)
    pooled_part = pool_windows(jax.nn.silu(skip_sum), keep_mask, WLEN)
    pooled = lax.all_gather(pooled_part, "chan", axis=1, tiled=True)
    nll_all, grad_pool = head_grads(
        pooled, event_bin, observed, head_w1, head_b1, head_w2, head_second_bias
    )
    nll_values = lax.dynamic_slice_in_dim(nll_all, chan_at * own_windows, own_windows, 0)
    pool_part = lax.dynamic_slice_in_dim(grad_pool, chan_at * chan_part, chan_part, 1)
    grad_skip = (spread_rows(pool_part, WLEN) * keep_mask[:, None] * silu_slope(skip_sum)).astype(
        jnp.bfloat16
    )
    skip_grads_all = lax.all_gather(grad_skip, "chan", axis=1, tiled=True)
    grad_rows = None
    for layer_number in range(layers - 1, -1, -1):
        tap_old = own_columns(tap_weight[layer_number, 0], chan_at, chan_part, width)
        tap_new = own_columns(tap_weight[layer_number, 1], chan_at, chan_part, width)
        skip_rows = lax.dynamic_slice_in_dim(
            skip_weight[layer_number], chan_at * chan_part, chan_part, 0
        )
        grad_gated = jnp.dot(skip_grads_all, skip_rows.T, preferred_element_type=jnp.float32)
        if grad_rows is not None:
            rows_all = lax.all_gather(grad_rows, "chan", axis=1, tiled=True)
            res_rows = lax.dynamic_slice_in_dim(
                res_weight[layer_number], chan_at * chan_part, chan_part, 0
            )
            grad_gated = grad_gated + jnp.dot(
                rows_all, res_rows.T, preferred_element_type=jnp.float32
            )
        preactivation_gradient = gate_grads(preacts[layer_number], grad_gated, chan_part)
        ahead = advance(preactivation_gradient, base_shift * 2**layer_number)
        partial_sum = jnp.dot(preactivation_gradient, tap_new.T, preferred_element_type=jnp.float32)
        partial_sum = partial_sum + jnp.dot(ahead, tap_old.T, preferred_element_type=jnp.float32)
        own_sum = lax.psum_scatter(
            partial_sum.astype(jnp.bfloat16), "chan", scatter_dimension=1, tiled=True
        ).astype(jnp.float32)
        if grad_rows is not None:
            own_sum = own_sum + grad_rows.astype(jnp.float32)
        grad_rows = own_sum.astype(jnp.bfloat16)
    return (nll_values, grad_rows)


def solution(mesh):
    return jax.shard_map(
        local,
        mesh=mesh,
        in_specs=(
            P("tm", "chan"),
            P("tm", "chan"),
            P(),
            P(),
            P(),
            P(),
            P(),
            P(),
            P(),
            P(),
            P("tm"),
            P("tm"),
            P(),
        ),
        out_specs=(P(("tm", "chan")), P("tm", "chan")),
        check_vma=False,
    )
```

profile of v0, /device:TPU:0, one launch (start us, length us, event | category | flops | bytes accessed | tf_op | source)
XLA Modules:
  0.0 238.0 jit_solution(4688544379573484493)
XLA Ops:
  7.2 7.6 %all_gather.39 = bf16[512,256]{1,0:T(8,128)(2,1)S(1)} all-gather(bf16[512,128]{1,0:T(8,128)(2,1)} %param.13), channel_id=1, replica_groups=mesh['tm'=16,'chan'=2] {'chan'}, dimensions={1}, use_global_device_ids=true | all-gather | bytes 393216 | tf_op jit(solution)/shard_map/all_gather | solution.py:124
  14.8 2.0 collective-permute-start
  17.4 1.2 multiply_log_fusion
  18.6 1.2 broadcast_compare_fusion
  20.5 0.9 fusion.121
  21.4 1.8 fusion.120
  23.2 1.8 fusion.119
  26.5 1.2 fusion.4
  27.8 6.3 %all_gather.40 = bf16[512,256]{0,1:T(8,128)(2,1)S(1)} all-gather(bf16[512,128]{0,1:T(8,128)(2,1)S(1)} %multiply_convert_fusion.11), channel_id=1, replica_groups=mesh['tm'=16,'chan'=2] {'chan'}, dimensions={1}, use_global_device_ids=true | all-gather | bytes 393216 | tf_op jit(solution)/shard_map/all_gather | solution.py:130
  34.4 6.6 %all_gather.41 = bf16[512,256]{1,0:T(8,128)(2,1)S(1)} all-gather(bf16[512,128]{1,0:T(8,128)(2,1)S(1)} %fusion.9), channel_id=1, replica_groups=mesh['tm'=16,'chan'=2] {'chan'}, dimensions={1}, use_global_device_ids=true | all-gather | bytes 393216 | tf_op jit(solution)/shard_map/all_gather | solution.py:124
  41.1 3.7 %collective-permute-start.1 = (bf16[512,256]{1,0:T(8,128)(2,1)S(1)}, bf16[512,256]{1,0:T(8,128)(2,1)S(1)}, u32[]{:S(2)}, u32[]{:S(2)}) collective-permute-start(bf16[512,256]{1,0:T(8,128)(2,1)S(1)} %all_gather.41), channel_id=1, source_target_pairs={{0,4},{2,6},{4,8},{6,10},{8,12},{10,14},{12,16},{14,18},{16,20},{1... | collective-permute-start | bytes 786440 | tf_op jit(solution)/shard_map/ppermute | solution.py:12
  45.3 4.8 %collective-permute-done.1 = bf16[512,256]{1,0:T(8,128)(2,1)S(1)} collective-permute-done((bf16[512,256]{1,0:T(8,128)(2,1)S(1)}, bf16[512,256]{1,0:T(8,128)(2,1)S(1)}, u32[]{:S(2)}, u32[]{:S(2)}) %collective-permute-start.1) | collective-permute-done | bytes 262176 | tf_op jit(solution)/shard_map/ppermute | solution.py:12
  50.5 5.6 %all_gather.42 = bf16[512,256]{0,1:T(8,128)(2,1)S(1)} all-gather(bf16[512,128]{0,1:T(8,128)(2,1)S(1)} %multiply_convert_fusion.10), channel_id=1, replica_groups=mesh['tm'=16,'chan'=2] {'chan'}, dimensions={1}, use_global_device_ids=true | all-gather | bytes 393216 | tf_op jit(solution)/shard_map/all_gather | solution.py:130
  56.4 5.7 %all_gather.43 = bf16[512,256]{1,0:T(8,128)(2,1)S(1)} all-gather(bf16[512,128]{1,0:T(8,128)(2,1)S(1)} %fusion.10), channel_id=1, replica_groups=mesh['tm'=16,'chan'=2] {'chan'}, dimensions={1}, use_global_device_ids=true | all-gather | bytes 393216 | tf_op jit(solution)/shard_map/all_gather | solution.py:124
  62.0 5.3 %collective-permute-start.2 = (bf16[512,256]{1,0:T(8,128)(2,1)S(1)}, bf16[512,256]{1,0:T(8,128)(2,1)S(1)}, u32[]{:S(2)}, u32[]{:S(2)}) collective-permute-start(bf16[512,256]{1,0:T(8,128)(2,1)S(1)} %all_gather.43), channel_id=1, source_target_pairs={{0,8},{2,10},{4,12},{6,14},{8,16},{10,18},{12,20},{14,22},{16,24},... | collective-permute-start | bytes 786440 | tf_op jit(solution)/shard_map/ppermute | solution.py:12
  67.9 3.3 %collective-permute-done.2 = bf16[512,256]{1,0:T(8,128)(2,1)S(1)} collective-permute-done((bf16[512,256]{1,0:T(8,128)(2,1)S(1)}, bf16[512,256]{1,0:T(8,128)(2,1)S(1)}, u32[]{:S(2)}, u32[]{:S(2)}) %collective-permute-start.2) | collective-permute-done | bytes 262176 | tf_op jit(solution)/shard_map/ppermute | solution.py:12
  71.6 6.3 %all_gather.44 = bf16[512,256]{0,1:T(8,128)(2,1)S(1)} all-gather(bf16[512,128]{0,1:T(8,128)(2,1)S(1)} %multiply_convert_fusion.9), channel_id=1, replica_groups=mesh['tm'=16,'chan'=2] {'chan'}, dimensions={1}, use_global_device_ids=true | all-gather | bytes 393216 | tf_op jit(solution)/shard_map/all_gather | solution.py:130
  78.2 5.7 %all_gather.45 = bf16[512,256]{1,0:T(8,128)(2,1)S(1)} all-gather(bf16[512,128]{1,0:T(8,128)(2,1)S(1)} %fusion.11), channel_id=1, replica_groups=mesh['tm'=16,'chan'=2] {'chan'}, dimensions={1}, use_global_device_ids=true | all-gather | bytes 393216 | tf_op jit(solution)/shard_map/all_gather | solution.py:124
  83.8 5.2 %collective-permute-start.3 = (bf16[512,256]{1,0:T(8,128)(2,1)S(1)}, bf16[512,256]{1,0:T(8,128)(2,1)S(1)}, u32[]{:S(2)}, u32[]{:S(2)}) collective-permute-start(bf16[512,256]{1,0:T(8,128)(2,1)S(1)} %all_gather.45), channel_id=1, source_target_pairs={{0,16},{2,18},{4,20},{6,22},{8,24},{10,26},{12,28},{14,30},{1,17},... | collective-permute-start | bytes 786440 | tf_op jit(solution)/shard_map/ppermute | solution.py:12
  89.6 3.4 %collective-permute-done.3 = bf16[512,256]{1,0:T(8,128)(2,1)S(1)} collective-permute-done((bf16[512,256]{1,0:T(8,128)(2,1)S(1)}, bf16[512,256]{1,0:T(8,128)(2,1)S(1)}, u32[]{:S(2)}, u32[]{:S(2)}) %collective-permute-start.3) | collective-permute-done | bytes 262176 | tf_op jit(solution)/shard_map/ppermute | solution.py:12
  93.4 6.0 %all_gather.46 = bf16[512,256]{0,1:T(8,128)(2,1)S(1)} all-gather(bf16[512,128]{0,1:T(8,128)(2,1)S(1)} %multiply_convert_fusion.8), channel_id=1, replica_groups=mesh['tm'=16,'chan'=2] {'chan'}, dimensions={1}, use_global_device_ids=true | all-gather | bytes 393216 | tf_op jit(solution)/shard_map/all_gather | solution.py:130
  99.4 1.0 multiply_multiply_fusion
  100.4 1.0 reshape.66
  103.1 4.9 %all_gather.47 = f32[4,256]{0,1:T(8,128)S(1)} all-gather(f32[4,128]{0,1:T(8,128)S(1)} %broadcast_divide_fusion), channel_id=1, replica_groups=mesh['tm'=16,'chan'=2] {'chan'}, dimensions={1}, use_global_device_ids=true | all-gather | bytes 6144 | tf_op jit(solution)/shard_map/all_gather | solution.py:146
  108.1 1.0 convolution_add_fusion.18
  110.0 0.9 fusion.117
  113.3 1.1 fusion.13
  114.4 5.6 %all_gather.48 = bf16[512,256]{0,1:T(8,128)(2,1)S(1)} all-gather(bf16[512,128]{0,1:T(8,128)(2,1)S(1)} %fusion.13), channel_id=1, replica_groups=mesh['tm'=16,'chan'=2] {'chan'}, dimensions={1}, use_global_device_ids=true | all-gather | bytes 393216 | tf_op jit(solution)/shard_map/all_gather | solution.py:155
  120.0 1.1 multiply_convert_fusion.7
  121.2 1.4 collective-permute-start.4
  122.9 7.6 %collective-permute-done.4 = bf16[512,256]{0,1:T(8,128)(2,1)S(1)} collective-permute-done((bf16[512,256]{0,1:T(8,128)(2,1)S(1)}, bf16[512,256]{0,1:T(8,128)(2,1)S(1)}, u32[]{:S(2)}, u32[]{:S(2)}) %collective-permute-start.4) | collective-permute-done | bytes 262176 | tf_op jit(solution)/shard_map/ppermute | solution.py:12
  131.7 12.7 %reduce-scatter.13.cloned.1.call-done = bf16[128,512]{1,0:T(8,128)(2,1)} async-done(((bf16[256,512]{1,0:T(8,128)(2,1)}), bf16[128,512]{1,0:T(8,128)(2,1)}) %reduce-scatter.13.cloned.1.call-update) | async-done | bytes 131088
  144.4 1.0 copy.38
  145.4 5.9 %all_gather.49 = bf16[512,256]{1,0:T(8,128)(2,1)S(1)} all-gather(bf16[512,128]{1,0:T(8,128)(2,1)S(1)} %copy.38), channel_id=1, replica_groups=mesh['tm'=16,'chan'=2] {'chan'}, dimensions={1}, use_global_device_ids=true | all-gather | bytes 393216 | tf_op jit(solution)/shard_map/all_gather | solution.py:165
  151.9 1.4 collective-permute-start.5
  153.6 7.5 %collective-permute-done.5 = bf16[512,256]{0,1:T(8,128)(2,1)S(1)} collective-permute-done((bf16[512,256]{0,1:T(8,128)(2,1)S(1)}, bf16[512,256]{0,1:T(8,128)(2,1)S(1)}, u32[]{:S(2)}, u32[]{:S(2)}) %collective-permute-start.5) | collective-permute-done | bytes 262176 | tf_op jit(solution)/shard_map/ppermute | solution.py:12
  162.3 10.9 %reduce-scatter.15.cloned.1.call-done = bf16[128,512]{1,0:T(8,128)(2,1)} async-done(((bf16[256,512]{1,0:T(8,128)(2,1)}), bf16[128,512]{1,0:T(8,128)(2,1)}) %reduce-scatter.15.cloned.1.call-update) | async-done | bytes 131088
  173.2 1.0 copy.40
  174.2 5.9 %all_gather.50 = bf16[512,256]{1,0:T(8,128)(2,1)S(1)} all-gather(bf16[512,128]{1,0:T(8,128)(2,1)S(1)} %add_convert_fusion.2), channel_id=1, replica_groups=mesh['tm'=16,'chan'=2] {'chan'}, dimensions={1}, use_global_device_ids=true | all-gather | bytes 393216 | tf_op jit(solution)/shard_map/all_gather | solution.py:165
  180.7 1.4 collective-permute-start.6
  182.4 7.5 %collective-permute-done.6 = bf16[512,256]{0,1:T(8,128)(2,1)S(1)} collective-permute-done((bf16[512,256]{0,1:T(8,128)(2,1)S(1)}, bf16[512,256]{0,1:T(8,128)(2,1)S(1)}, u32[]{:S(2)}, u32[]{:S(2)}) %collective-permute-start.6) | collective-permute-done | bytes 262176 | tf_op jit(solution)/shard_map/ppermute | solution.py:12
  191.1 11.8 %reduce-scatter.17.cloned.1.call-done = bf16[128,512]{1,0:T(8,128)(2,1)} async-done(((bf16[256,512]{1,0:T(8,128)(2,1)}), bf16[128,512]{1,0:T(8,128)(2,1)}) %reduce-scatter.17.cloned.1.call-update) | async-done | bytes 131088
  202.9 1.0 copy.42
  204.0 6.0 %all_gather.51 = bf16[512,256]{1,0:T(8,128)(2,1)S(1)} all-gather(bf16[512,128]{1,0:T(8,128)(2,1)S(1)} %add_convert_fusion.1), channel_id=1, replica_groups=mesh['tm'=16,'chan'=2] {'chan'}, dimensions={1}, use_global_device_ids=true | all-gather | bytes 393216 | tf_op jit(solution)/shard_map/all_gather | solution.py:165
  210.5 1.3 collective-permute-start.7
  212.0 1.9 collective-permute-done.7
  215.6 14.1 %reduce-scatter.19.cloned.1.call-done = bf16[128,512]{1,0:T(8,128)(2,1)} async-done(((bf16[256,512]{1,0:T(8,128)(2,1)}), bf16[128,512]{1,0:T(8,128)(2,1)}) %reduce-scatter.19.cloned.1.call-update) | async-done | bytes 131088
  229.7 1.0 copy.44
  (133 shorter events, 19.3 us)
Async XLA Ops:
  7.2 100.9 %copy-start = (f32[256,256]{1,0:T(8,128)S(1)}, f32[256,256]{1,0:T(8,128)}, u32[]{:S(2)}) copy-start(f32[256,256]{1,0:T(8,128)} %param.19) | copy-start | bytes 786436
  7.2 17.9 %copy-start.1 = (bf16[4,2,256,512]{3,2,1,0:T(8,128)(2,1)S(1)}, bf16[4,2,256,512]{3,2,1,0:T(8,128)(2,1)}, u32[]{:S(2)}) copy-start(bf16[4,2,256,512]{3,2,1,0:T(8,128)(2,1)} %param.15) | copy-start | bytes 6291460
  7.2 137.2 %reduce-scatter.13.cloned.1.call-start = ((), (), s32[]{:S(2)}) async-start(), calls=%async_computation.4 | async-start | bytes 393216
  14.8 11.7 %collective-permute-start = (bf16[512,256]{1,0:T(8,128)(2,1)S(1)}, bf16[512,256]{1,0:T(8,128)(2,1)}, u32[]{:S(2)}, u32[]{:S(2)}) collective-permute-start(bf16[512,256]{1,0:T(8,128)(2,1)S(1)} %all_gather.39), channel_id=1, source_target_pairs={{0,2},{2,4},{4,6},{6,8},{8,10},{10,12},{12,14},{14,16},{16,18},{18... | collective-permute-start | bytes 786440 | tf_op jit(solution)/shard_map/ppermute | solution.py:12
  20.5 78.9 %copy-start.22 = (f32[512]{0:T(512)}, f32[512]{0:T(512)S(1)}, u32[]{:S(2)}) copy-start(f32[512]{0:T(512)S(1)} %fusion.97) | copy-start | bytes 6148
  25.0 74.3 %copy-start.20 = (bf16[1,256,256]{2,1,0:T(8,128)(2,1)}, bf16[1,256,256]{2,1,0:T(8,128)(2,1)S(1)}, u32[]{:S(2)}) copy-start(bf16[1,256,256]{2,1,0:T(8,128)(2,1)S(1)} %get-tuple-element.20) | copy-start | bytes 393220
  25.2 0.9 copy-start.19
  25.4 24.6 %copy-start.2 = (bf16[256,128]{1,0:T(8,128)(2,1)}, bf16[256,128]{1,0:T(8,128)(2,1)S(1)}, u32[]{:S(2)}) copy-start(bf16[256,128]{1,0:T(8,128)(2,1)S(1)} %get-tuple-element.62) | copy-start | bytes 196612
  25.4 24.6 %copy-start.4 = (bf16[256,128]{1,0:T(8,128)(2,1)}, bf16[256,128]{1,0:T(8,128)(2,1)S(1)}, u32[]{:S(2)}) copy-start(bf16[256,128]{1,0:T(8,128)(2,1)S(1)} %get-tuple-element.63) | copy-start | bytes 196612
  25.4 8.7 %copy-start.6 = (bf16[512,128]{1,0:T(8,128)(2,1)S(1)}, bf16[512,128]{1,0:T(8,128)(2,1)}, u32[]{:S(2)}) copy-start(bf16[512,128]{1,0:T(8,128)(2,1)} %param.13) | copy-start | bytes 393220
  25.5 8.7 %copy-start.7 = (bf16[1,256,256]{2,1,0:T(8,128)(2,1)S(1)}, bf16[1,256,256]{2,1,0:T(8,128)(2,1)}, u32[]{:S(2)}) copy-start(bf16[1,256,256]{2,1,0:T(8,128)(2,1)} %get-tuple-element.25) | copy-start | bytes 393220
  26.2 18.6 %copy-start.13 = (bf16[1,256,256]{2,1,0:T(8,128)(2,1)S(1)}, bf16[1,256,256]{2,1,0:T(8,128)(2,1)}, u32[]{:S(2)}) copy-start(bf16[1,256,256]{2,1,0:T(8,128)(2,1)} %get-tuple-element.22) | copy-start | bytes 393220
  41.1 15.0 %copy-start.9 = (bf16[1,256,256]{2,1,0:T(8,128)(2,1)S(1)}, bf16[1,256,256]{2,1,0:T(8,128)(2,1)}, u32[]{:S(2)}) copy-start(bf16[1,256,256]{2,1,0:T(8,128)(2,1)} %get-tuple-element.26) | copy-start | bytes 393220
  41.1 9.0 %collective-permute-start.1 = (bf16[512,256]{1,0:T(8,128)(2,1)S(1)}, bf16[512,256]{1,0:T(8,128)(2,1)S(1)}, u32[]{:S(2)}, u32[]{:S(2)}) collective-permute-start(bf16[512,256]{1,0:T(8,128)(2,1)S(1)} %all_gather.41), channel_id=1, source_target_pairs={{0,4},{2,6},{4,8},{6,10},{8,12},{10,14},{12,16},{14,18},{16,20},{1... | collective-permute-start | bytes 786440 | tf_op jit(solution)/shard_map/ppermute | solution.py:12
  45.0 22.3 %copy-start.15 = (bf16[1,256,256]{2,1,0:T(8,128)(2,1)S(1)}, bf16[1,256,256]{2,1,0:T(8,128)(2,1)}, u32[]{:S(2)}) copy-start(bf16[1,256,256]{2,1,0:T(8,128)(2,1)} %get-tuple-element.21) | copy-start | bytes 393220
  62.0 9.1 %collective-permute-start.2 = (bf16[512,256]{1,0:T(8,128)(2,1)S(1)}, bf16[512,256]{1,0:T(8,128)(2,1)S(1)}, u32[]{:S(2)}, u32[]{:S(2)}) collective-permute-start(bf16[512,256]{1,0:T(8,128)(2,1)S(1)} %all_gather.43), channel_id=1, source_target_pairs={{0,8},{2,10},{4,12},{6,14},{8,16},{10,18},{12,20},{14,22},{16,24},... | collective-permute-start | bytes 786440 | tf_op jit(solution)/shard_map/ppermute | solution.py:12
  67.3 10.5 %copy-start.11 = (bf16[1,256,256]{2,1,0:T(8,128)(2,1)S(1)}, bf16[1,256,256]{2,1,0:T(8,128)(2,1)}, u32[]{:S(2)}) copy-start(bf16[1,256,256]{2,1,0:T(8,128)(2,1)} %get-tuple-element.24) | copy-start | bytes 393220
  67.6 21.5 %copy-start.17 = (bf16[1,256,256]{2,1,0:T(8,128)(2,1)S(1)}, bf16[1,256,256]{2,1,0:T(8,128)(2,1)}, u32[]{:S(2)}) copy-start(bf16[1,256,256]{2,1,0:T(8,128)(2,1)} %get-tuple-element.23) | copy-start | bytes 393220
  83.8 9.1 %collective-permute-start.3 = (bf16[512,256]{1,0:T(8,128)(2,1)S(1)}, bf16[512,256]{1,0:T(8,128)(2,1)S(1)}, u32[]{:S(2)}, u32[]{:S(2)}) collective-permute-start(bf16[512,256]{1,0:T(8,128)(2,1)S(1)} %all_gather.45), channel_id=1, source_target_pairs={{0,16},{2,18},{4,20},{6,22},{8,24},{10,26},{12,28},{14,30},{1,17},... | collective-permute-start | bytes 786440 | tf_op jit(solution)/shard_map/ppermute | solution.py:12
  93.2 15.8 %copy-start.21 = (f32[256,12]{0,1:T(8,128)S(1)}, f32[256,12]{0,1:T(8,128)}, u32[]{:S(2)}) copy-start(f32[256,12]{0,1:T(8,128)} %param.21) | copy-start | bytes 36868
  121.1 30.2 %copy-start.12 = (bf16[1,256,256]{2,1,0:T(8,128)(2,1)S(1)}, bf16[1,256,256]{2,1,0:T(8,128)(2,1)}, u32[]{:S(2)}) copy-start(bf16[1,256,256]{2,1,0:T(8,128)(2,1)} %get-tuple-element.24) | copy-start | bytes 393220
  121.2 30.4 %copy-start.18 = (bf16[1,256,256]{2,1,0:T(8,128)(2,1)S(1)}, bf16[1,256,256]{2,1,0:T(8,128)(2,1)}, u32[]{:S(2)}) copy-start(bf16[1,256,256]{2,1,0:T(8,128)(2,1)} %get-tuple-element.23) | copy-start | bytes 393220
  121.2 9.3 %collective-permute-start.4 = (bf16[512,256]{0,1:T(8,128)(2,1)S(1)}, bf16[512,256]{0,1:T(8,128)(2,1)S(1)}, u32[]{:S(2)}, u32[]{:S(2)}) collective-permute-start(bf16[512,256]{0,1:T(8,128)(2,1)S(1)} %pad_maximum_fusion), channel_id=1, source_target_pairs={{16,0},{18,2},{20,4},{22,6},{24,8},{26,10},{28,12},{30,14},{17,1},... | collective-permute-start | bytes 786440 | tf_op jit(solution)/shard_map/ppermute | solution.py:12
  131.6 41.5 %reduce-scatter.15.cloned.1.call-start = ((), (), s32[]{:S(2)}) async-start(), calls=%async_computation.5 | async-start | bytes 393216
  151.9 28.3 %copy-start.10 = (bf16[1,256,256]{2,1,0:T(8,128)(2,1)S(1)}, bf16[1,256,256]{2,1,0:T(8,128)(2,1)}, u32[]{:S(2)}) copy-start(bf16[1,256,256]{2,1,0:T(8,128)(2,1)} %get-tuple-element.26) | copy-start | bytes 393220
  151.9 28.5 %copy-start.16 = (bf16[1,256,256]{2,1,0:T(8,128)(2,1)S(1)}, bf16[1,256,256]{2,1,0:T(8,128)(2,1)}, u32[]{:S(2)}) copy-start(bf16[1,256,256]{2,1,0:T(8,128)(2,1)} %get-tuple-element.21) | copy-start | bytes 393220
  151.9 9.2 %collective-permute-start.5 = (bf16[512,256]{0,1:T(8,128)(2,1)S(1)}, bf16[512,256]{0,1:T(8,128)(2,1)S(1)}, u32[]{:S(2)}, u32[]{:S(2)}) collective-permute-start(bf16[512,256]{0,1:T(8,128)(2,1)S(1)} %pad_maximum_fusion.1), channel_id=1, source_target_pairs={{8,0},{10,2},{12,4},{14,6},{16,8},{18,10},{20,12},{22,14},{24,16},... | collective-permute-start | bytes 786440 | tf_op jit(solution)/shard_map/ppermute | solution.py:12
  162.2 40.6 %reduce-scatter.17.cloned.1.call-start = ((), (), s32[]{:S(2)}) async-start(), calls=%async_computation.6 | async-start | bytes 393216
  180.2 9.8 %copy-start.3 = (bf16[256,128]{1,0:T(8,128)(2,1)S(1)}, bf16[256,128]{1,0:T(8,128)(2,1)}, u32[]{:S(2)}) copy-start(bf16[256,128]{1,0:T(8,128)(2,1)} %copy-done.2) | copy-start | bytes 196612
  180.2 9.8 %copy-start.5 = (bf16[256,128]{1,0:T(8,128)(2,1)S(1)}, bf16[256,128]{1,0:T(8,128)(2,1)}, u32[]{:S(2)}) copy-start(bf16[256,128]{1,0:T(8,128)(2,1)} %copy-done.4) | copy-start | bytes 196612
  180.7 29.2 %copy-start.8 = (bf16[1,256,256]{2,1,0:T(8,128)(2,1)S(1)}, bf16[1,256,256]{2,1,0:T(8,128)(2,1)}, u32[]{:S(2)}) copy-start(bf16[1,256,256]{2,1,0:T(8,128)(2,1)} %get-tuple-element.25) | copy-start | bytes 393220
  180.7 29.4 %copy-start.14 = (bf16[1,256,256]{2,1,0:T(8,128)(2,1)S(1)}, bf16[1,256,256]{2,1,0:T(8,128)(2,1)}, u32[]{:S(2)}) copy-start(bf16[1,256,256]{2,1,0:T(8,128)(2,1)} %get-tuple-element.22) | copy-start | bytes 393220
  180.7 9.2 %collective-permute-start.6 = (bf16[512,256]{0,1:T(8,128)(2,1)S(1)}, bf16[512,256]{0,1:T(8,128)(2,1)S(1)}, u32[]{:S(2)}, u32[]{:S(2)}) collective-permute-start(bf16[512,256]{0,1:T(8,128)(2,1)S(1)} %pad_maximum_fusion.2), channel_id=1, source_target_pairs={{4,0},{6,2},{8,4},{10,6},{12,8},{14,10},{16,12},{18,14},{20,16},{2... | collective-permute-start | bytes 786440 | tf_op jit(solution)/shard_map/ppermute | solution.py:12
  191.1 38.7 %reduce-scatter.19.cloned.1.call-start = ((), (), s32[]{:S(2)}) async-start(), calls=%async_computation.7 | async-start | bytes 393216
  210.4 4.6 %copy-start.23 = (f32[4]{0:T(128)S(1)}, f32[4]{0:T(128)}, u32[]{:S(2)}) copy-start(f32[4]{0:T(128)} %get-tuple-element.59) | copy-start | bytes 52
  210.5 3.4 %collective-permute-start.7 = (bf16[512,256]{0,1:T(8,128)(2,1)S(1)}, bf16[512,256]{0,1:T(8,128)(2,1)S(1)}, u32[]{:S(2)}, u32[]{:S(2)}) collective-permute-start(bf16[512,256]{0,1:T(8,128)(2,1)S(1)} %pad_maximum_fusion.3), channel_id=1, source_target_pairs={{2,0},{4,2},{6,4},{8,6},{10,8},{12,10},{14,12},{16,14},{18,16},{20... | collective-permute-start | bytes 786440 | tf_op jit(solution)/shard_map/ppermute | solution.py:12
Sparse Core Ops, SparseCore 0:
  131.7 12.6 reduce-scatter.12
  162.4 10.7 reduce-scatter.14
  191.2 11.6 reduce-scatter.16
  215.1 14.5 reduce-scatter.18
where the time goes:
time: 239 us; the launch traced here: 238 us
  waiting for transfers between devices  85.4 us (36%)
  blocking collectives  78.2 us (33%)
  starting transfers between devices  21.9 us (9%)
  local copies, waits for them, and re-layouts  15.1 us (6%)
  between operations  15.1 us (6%)
  matrix products  12.6 us (5%)
  other arithmetic  9.65 us (4%)
    unnamed x8, waiting for transfers between devices  49.5 us
    ppermute x8, waiting for transfers between devices, passed_along(): return lax.ppermute(block, axis, route)  35.9 us
    all_gather x4, blocking collectives, local(): whole = lax.all_gather(current, 'chan', axis=1, tiled=True)  25.5 us
    all_gather x4, blocking collectives, local(): gated_all = lax.all_gather(gated, 'chan', axis=1, tiled=True)  24.2 us
    ppermute x8, starting transfers between devices, passed_along(): return lax.ppermute(block, axis, route)  21.7 us
    all_gather x3, blocking collectives, local(): rows_all = lax.all_gather(grad_rows, 'chan', axis=1, tiled=True)  17.8 us
    unnamed x57, local copies, waits for them, and re-layouts  8.2 us
    all_gather x1, blocking collectives, local(): skip_grads_all = lax.all_gather(grad_skip, 'chan', axis=1, tiled=True)  5.64 us
  transfers between devices with their start and end apart: 12, of which 11 were waited for; matrix products, arithmetic and copies ran while one was open for 5% of the time, Pallas kernels for 0%

commit v1 on v0

v1 whole, which is shorter than its diff:
```python
import functools

import jax
import jax.numpy as jnp
from jax import lax
from jax.experimental import pallas as pl
from jax.experimental.pallas import tpu as pltpu
from jax.sharding import PartitionSpec as P

WLEN = 128
MESH = pl.DeviceIdType.MESH
F32 = jnp.float32
BF16 = jnp.bfloat16
X_PART, SKIP_PART, OLD_SAME, OLD_CROSS, X_NEXT, B_BACK, B0_SAME, B0_CROSS, A_CROSS = 0, 1, 2, 3, 4, 7, 10, 11, 12
ITEMS = 13


def mm(a, b):
    return jnp.dot(a, b, preferred_element_type=F32)


def mm_t(a, b, precision=None):
    return lax.dot_general(a, b, (((1,), (1,)), ((), ())), precision=precision, preferred_element_type=F32)


def sigmoid(v):
    return 0.5 * jnp.tanh(0.5 * v) + 0.5


def head(pooled, bin_at, flag, w1, b1, w2, b2):
    best = lax.Precision.HIGHEST
    pre = jnp.dot(pooled, w1, precision=best, preferred_element_type=F32) + b1
    sig = jax.nn.sigmoid(pre)
    hidden = pre * sig
    mixes = w2.shape[1] // 3
    parts = [w2[:, i * mixes : (i + 1) * mixes] for i in range(3)]
    p_l, p_s, p_k = (
        jnp.dot(hidden, parts[i], precision=best, preferred_element_type=F32) + b2[:, i * mixes : (i + 1) * mixes]
        for i in range(3)
    )
    tan_l, log_scale, tan_k = jnp.tanh(p_l), jnp.tanh(p_s), jnp.tanh(p_k)
    logits, log_shape = 4.0 * tan_l, 0.5 * tan_k
    log_pi = logits - jnp.log(jnp.sum(jnp.exp(logits), axis=1, keepdims=True))
    shape_value = jnp.exp(log_shape)
    log_time = jnp.log(jnp.full(p_l.shape, (bin_at.astype(F32) + 1.0) / 8.0, F32))
    seen = jnp.full(p_l.shape, flag, jnp.int32) == 1
    seen_one = jnp.where(seen, 1.0, 0.0)
    ratio = log_time - log_scale
    power = jnp.exp(shape_value * ratio)
    density = log_shape - log_scale + (shape_value - 1.0) * ratio - power
    terms = jnp.exp(log_pi + jnp.where(seen, density, -power))
    total = jnp.sum(terms, axis=1, keepdims=True)
    nll = -jnp.log(total)
    share = terms / total
    d_l = (jnp.exp(log_pi) - share) * 4.0 * (1.0 - tan_l * tan_l)
    d_s = -share * shape_value * (power - seen_one) * (1.0 - log_scale * log_scale)
    d_k = -share * (seen_one + shape_value * ratio * (seen_one - power)) * 0.5 * (1.0 - tan_k * tan_k)
    d_hidden = mm_t(d_l, parts[0], best) + mm_t(d_s, parts[1], best) + mm_t(d_k, parts[2], best)
    d_pre = d_hidden * sig * (1.0 + pre * (1.0 - sig))
    return nll, mm_t(d_pre, w1, best)


def kernel(
    n, layers, windows,
    signal, skip_in, tap, bias, res, skw, w1, b1, w2, b2, bins, flags, limit,
    nll_ref, out_ref,
    xin, skin, old0, xs, olds, tan_f, sig_a, skips, bsend, brecv, b0send, b0recv, a_own, a_send, a_recv, send_sem, recv_sem,
):
    me, c = lax.axis_index("tm"), lax.axis_index("chan")
    other = 1 - c
    half = windows * WLEN
    part = signal.shape[1]
    shifts = [n // 16 * 2**k for k in range(layers)]

    barrier = pltpu.get_barrier_semaphore()
    expected = jnp.int32(1)
    pl.semaphore_signal(barrier, inc=1, device_id=(me, other), device_id_type=MESH)
    for k, shift in enumerate(shifts):
        for target, ok in ((me + shift, me + shift < n), (me - shift, me >= shift)):
            lanes = (c, other) if k == 0 else (c,)
            for lane in lanes:

                @pl.when(ok)
                def _(target=target, lane=lane):
                    pl.semaphore_signal(barrier, inc=1, device_id=(target, lane), device_id_type=MESH)

            expected = expected + jnp.where(ok, len(lanes), 0).astype(jnp.int32)
    pl.semaphore_wait(barrier, expected)

    def copy(src, dst, item, j, tm_to, lane):
        return pltpu.make_async_remote_copy(
            src_ref=src, dst_ref=dst, send_sem=send_sem.at[item, j], recv_sem=recv_sem.at[item, j],
            device_id=(tm_to, lane), device_id_type=MESH,
        )

    sends = []

    def send(cond, *args):
        sends.append((cond, args))
        if cond is None:
            copy(*args).start()
        else:

            @pl.when(cond)
            def _():
                copy(*args).start()

    def await_in(cond, dst, item, j):
        def wait():
            copy(dst, dst, item, j, me, other).wait_recv()

        if cond is None:
            wait()
        else:
            pl.when(cond)(wait)

    def later(k):
        return me + shifts[k] < n

    def earlier(k):
        return me >= shifts[k]

    def own_rows(j):
        return pl.ds(pl.multiple_of(c * half + j * WLEN, WLEN), WLEN)

    def other_rows(j):
        return pl.ds(pl.multiple_of(other * half + j * WLEN, WLEN), WLEN)

    chunks = range(windows)
    for j in chunks:
        send(None, signal.at[other_rows(j), :], xin.at[c, j], X_PART, j, me, other)
        send(later(0), signal.at[own_rows(j), :], old0.at[c, j], OLD_SAME, j, me + shifts[0], c)
        send(later(0), signal.at[other_rows(j), :], old0.at[c, j], OLD_CROSS, j, me + shifts[0], other)
    for j in chunks:
        send(None, skip_in.at[other_rows(j), :], skin.at[c, j], SKIP_PART, j, me, other)

    for j in chunks:
        xin[c, j] = signal[own_rows(j), :]
        skin[c, j] = skip_in[own_rows(j), :]

    @pl.when(me < shifts[0])
    def _():
        old0[...] = jnp.zeros_like(old0)

    @pl.when(me + shifts[0] >= n)
    def _():
        b0recv[...] = jnp.zeros_like(b0recv)

    for k in range(1, layers):

        @pl.when(me < shifts[k])
        def _(k=k):
            olds[k - 1] = jnp.zeros(olds.shape[1:], BF16)

        @pl.when(me + shifts[k] >= n)
        def _(k=k):
            brecv[k - 1] = jnp.zeros(brecv.shape[1:], BF16)

    width = part * 2
    fresh = {}
    for j in chunks:
        await_in(None, xin.at[other, j], X_PART, j)
        x = jnp.concatenate([xin[0, j], xin[1, j]], axis=1)
        fresh[j] = (x, mm(x, tap[0, 1]) + bias[0:1, :])

    def forward(k, j):
        x, pre = fresh[j]
        if k == 0:
            await_in(earlier(0), old0.at[c, j], OLD_SAME, j)
            await_in(earlier(0), old0.at[other, j], OLD_CROSS, j)
            old = jnp.concatenate([old0[0, j], old0[1, j]], axis=1)
        else:
            await_in(earlier(k), olds.at[k - 1, j], X_NEXT + k - 1, j)
            old = olds[k - 1, j]
        pre = pre + mm(old, tap[k, 0])
        fil, gate = jnp.tanh(pre[:, :width]), sigmoid(pre[:, width:])
        z = (fil * gate).astype(BF16)
        if k < layers - 1:
            x = (x.astype(F32) + mm(z, res[k])).astype(BF16)
            xs[k, j] = x
            send(later(k + 1), xs.at[k, j], olds.at[k, j], X_NEXT + k, j, me + shifts[k + 1], c)
        tan_f[k, j] = fil
        sig_a[k, j] = gate
        if k == 0:
            await_in(None, skin.at[other, j], SKIP_PART, j)
            base = jnp.concatenate([skin[0, j], skin[1, j]], axis=1).astype(F32)
        else:
            base = skips[j]
        skips[j] = base + mm(z, skw[k])
        if k < layers - 1:
            fresh[j] = (x, mm(x, tap[k + 1, 1]) + bias[k + 1 : k + 2, :])

    for k in range(layers):
        for j in chunks:
            forward(k, j)

    grads = {}
    own_terms = {}

    def loss(j):
        s = skips[j]
        first = me * 2 * half + c * half + j * WLEN
        rows = first + lax.broadcasted_iota(jnp.int32, (WLEN, 1), 0)
        last = limit[0]
        keep = jnp.where(rows < last, 1.0, 0.0)
        sig = sigmoid(s)
        count = jnp.clip(last - first, 0, WLEN).astype(F32)
        pooled = jnp.sum(s * sig * keep, axis=0, keepdims=True) / jnp.maximum(count, 1.0)
        at = c * windows + j
        nll, grad = head(
            jnp.broadcast_to(pooled, (8, width)), bins[at], flags[at], w1[...], b1[...], w2[...], b2[...]
        )
        nll_ref[j : j + 1, :] = jnp.broadcast_to(nll[0:1, :], (1, nll_ref.shape[1]))
        grads[j] = (grad[0:1, :] * keep * (sig * (1.0 + s * (1.0 - sig)))).astype(BF16)

    def backward(k, j):
        if k == layers - 1:
            loss(j)
        grad_z = mm_t(grads[j], skw[k])
        above = None
        if k < layers - 1:
            await_in(later(k + 1), brecv.at[k, j], B_BACK + k, j)
            above = (own_terms[j] + brecv[k, j].astype(F32)).astype(BF16)
            grad_z = grad_z + mm_t(above, res[k])
        fil, gate = tan_f[k, j], sig_a[k, j]
        through = grad_z * gate
        grad_pre = jnp.concatenate(
            [through * (1.0 - fil * fil), through * fil * (1.0 - gate)], axis=1
        ).astype(BF16)
        back = mm_t(grad_pre, tap[k, 0]).astype(BF16)
        if k > 0:
            bsend[k - 1, j] = back
            send(earlier(k), bsend.at[k - 1, j], brecv.at[k - 1, j], B_BACK + k - 1, j, me - shifts[k], c)
        else:
            b0send[0, j] = back[:, :part]
            b0send[1, j] = back[:, part:]
            send(earlier(0), b0send.at[c, j], b0recv.at[c, j], B0_SAME, j, me - shifts[0], c)
            send(earlier(0), b0send.at[other, j], b0recv.at[c, j], B0_CROSS, j, me - shifts[0], other)
        own = mm_t(grad_pre, tap[k, 1])
        if above is not None:
            own = own + above.astype(F32)
        if k > 0:
            own_terms[j] = own
        else:
            a_own[0, j], a_own[1, j] = own[:, :part], own[:, part:]
            low = own.astype(BF16)
            a_send[0, j], a_send[1, j] = low[:, :part], low[:, part:]
            send(None, a_send.at[other, j], a_recv.at[j], A_CROSS, j, me, other)

    for k in range(layers - 1, -1, -1):
        for j in chunks:
            backward(k, j)

    for j in chunks:
        await_in(later(0), b0recv.at[c, j], B0_SAME, j)
        out_ref[own_rows(j), :] = (a_own[c, j] + b0recv[c, j].astype(F32)).astype(BF16)
        await_in(None, a_recv.at[j], A_CROSS, j)
        await_in(later(0), b0recv.at[other, j], B0_CROSS, j)
        out_ref[other_rows(j), :] = (a_recv[j].astype(F32) + b0recv[other, j].astype(F32)).astype(BF16)

    for cond, args in sends:
        if cond is None:
            copy(*args).wait_send()
        else:

            @pl.when(cond)
            def _(args=args):
                copy(*args).wait_send()


def local(
    signal, skip_in, tap_weight, tap_bias, res_weight, skip_weight,
    head_w1, head_b1, head_w2, head_second_bias, event_bin, observed, valid_len,
):
    n = lax.axis_size("tm")
    layers = tap_weight.shape[0]
    rows, part = signal.shape
    windows = rows // WLEN // 2
    width = 2 * part
    vmem = pl.BlockSpec(memory_space=pltpu.VMEM)
    smem = pl.BlockSpec(memory_space=pltpu.SMEM)
    flops = 2 * windows * WLEN * width * width * (6 * layers + 6 * layers)
    nll, grad = pl.pallas_call(
        functools.partial(kernel, n, layers, windows),
        out_shape=(
            jax.ShapeDtypeStruct((windows, 128), F32),
            jax.ShapeDtypeStruct((rows, part), BF16),
        ),
        in_specs=[vmem] * 10 + [smem] * 3,
        out_specs=(vmem, vmem),
        scratch_shapes=[
            pltpu.VMEM((2, windows, WLEN, part), BF16),
            pltpu.VMEM((2, windows, WLEN, part), BF16),
            pltpu.VMEM((2, windows, WLEN, part), BF16),
            pltpu.VMEM((layers - 1, windows, WLEN, width), BF16),
            pltpu.VMEM((layers - 1, windows, WLEN, width), BF16),
            pltpu.VMEM((layers, windows, WLEN, width), F32),
            pltpu.VMEM((layers, windows, WLEN, width), F32),
            pltpu.VMEM((windows, WLEN, width), F32),
            pltpu.VMEM((layers - 1, windows, WLEN, width), BF16),
            pltpu.VMEM((layers - 1, windows, WLEN, width), BF16),
            pltpu.VMEM((2, windows, WLEN, part), BF16),
            pltpu.VMEM((2, windows, WLEN, part), BF16),
            pltpu.VMEM((2, windows, WLEN, part), F32),
            pltpu.VMEM((2, windows, WLEN, part), BF16),
            pltpu.VMEM((windows, WLEN, part), BF16),
            pltpu.SemaphoreType.DMA((ITEMS, windows)),
            pltpu.SemaphoreType.DMA((ITEMS, windows)),
        ],
        compiler_params=pltpu.CompilerParams(
            collective_id=0, has_side_effects=True, vmem_limit_bytes=40 * 1024 * 1024
        ),
        cost_estimate=pl.CostEstimate(flops=flops, bytes_accessed=4 * 1024 * 1024, transcendentals=0),
    )(
        signal, skip_in, tap_weight, tap_bias, res_weight, skip_weight,
        head_w1, head_b1[None, :], head_w2, head_second_bias[None, :], event_bin, observed, valid_len,
    )
    return nll[:, 0], grad


def solution(mesh):
    return jax.shard_map(
        local,
        mesh=mesh,
        in_specs=(
            P("tm", "chan"), P("tm", "chan"), P(), P(), P(), P(), P(), P(), P(), P(), P("tm"), P("tm"), P(),
        ),
        out_specs=(P(("tm", "chan")), P("tm", "chan")),
        check_vma=False,
    )
```

time: 239 us -> 58.7 us (0.25)
  waiting for transfers between devices: 85.4 us -> 0 us
  blocking collectives: 78.2 us -> 0 us
  Pallas kernels: 0 us -> 45.1 us
  starting transfers between devices: 21.9 us -> 0 us
  between operations: 15.1 us -> 1.3 us
  matrix products: 12.6 us -> 0 us
  other arithmetic: 9.65 us -> 0 us
  local copies, waits for them, and re-layouts: 15.1 us -> 11.8 us
    all_gather x13 -> x0, blocking collectives: 78.2 us -> none  [the longest x4 25.5 us: local(): whole = lax.all_gather(current, 'chan', axis=1, tiled=True)]
    unnamed x8 -> x0, waiting for transfers between devices: 49.5 us -> none
    pallas_call x0 -> x1, Pallas kernels: none -> 45.1 us  [local(): pl.pallas_call(functools.partial(kernel, n, layers, windows), out_shape=(...]
    ppermute x8 -> x0, waiting for transfers between devices: 35.9 us -> none  [passed_along(): return lax.ppermute(block, axis, route)]
    ppermute x8 -> x0, starting transfers between devices: 21.7 us -> none  [passed_along(): return lax.ppermute(block, axis, route)]
    dot_general x34 -> x0, matrix products: 12.6 us -> none  [the longest x4 2.05 us: local(): preact = jnp.dot(delayed, tap_old, preferred_element_type=jnp.float32)]
    slice x4 -> x1, local copies, waits for them, and re-layouts: 4.63 us -> 0.63 us  [local(): return (nll[:, 0], grad)]
    unnamed x57 -> x24, local copies, waits for them, and re-layouts: 8.2 us -> 11.2 us
  transfers between devices with their start and end apart: 12 -> 0, of which waited for: 11 -> 0; matrix products, arithmetic and copies ran while one was open for 5% -> 0% of each run, Pallas kernels for 0% -> 0%
where the time goes in v1:
time: 58.7 us; the launch traced here: 58.2 us
  Pallas kernels  45.1 us (77%)
  local copies, waits for them, and re-layouts  11.8 us (20%)
  between operations  1.3 us (2%)
    pallas_call x1, Pallas kernels, local(): pl.pallas_call(functools.partial(kernel, n, layers, windows), out_shape=(...  45.1 us
    unnamed x24, local copies, waits for them, and re-layouts  11.2 us

profile of v1, /device:TPU:0, one launch (start us, length us, event | category | flops | bytes accessed | tf_op | source)
XLA Modules:
  0.0 58.2 jit_solution(17787669548308018711)
XLA Ops:
  1.3 0.8 %copy.16.w2 = f32[256,12]{1,0:T(8,128)S(1)} copy(f32[256,12]{0,1:T(8,128)} %param.21) | data formatting | bytes 24576 | tf_op args[8]
  2.1 0.0 copy-start
  2.1 1.6 %copy-done = bf16[4,2,256,512]{3,2,1,0:T(8,128)(2,1)S(1)} copy-done((bf16[4,2,256,512]{3,2,1,0:T(8,128)(2,1)S(1)}, bf16[4,2,256,512]{3,2,1,0:T(8,128)(2,1)}, u32[]{:S(2)}) %copy-start) | copy-done | bytes 2097176
  3.7 0.0 copy-start.1
  3.7 1.0 %copy-done.1 = bf16[4,256,256]{2,1,0:T(8,128)(2,1)S(1)} copy-done((bf16[4,256,256]{2,1,0:T(8,128)(2,1)S(1)}, bf16[4,256,256]{2,1,0:T(8,128)(2,1)}, u32[]{:S(2)}) %copy-start.1) | copy-done | bytes 524312
  4.7 0.0 copy-start.2
  4.7 1.0 %copy-done.2 = bf16[3,256,256]{2,1,0:T(8,128)(2,1)S(1)} copy-done((bf16[3,256,256]{2,1,0:T(8,128)(2,1)S(1)}, bf16[3,256,256]{2,1,0:T(8,128)(2,1)}, u32[]{:S(2)}) %copy-start.2) | copy-done | bytes 393240
  5.7 0.0 copy-start.3
  5.7 0.9 %copy-done.3 = f32[256,256]{1,0:T(8,128)S(1)} copy-done((f32[256,256]{1,0:T(8,128)S(1)}, f32[256,256]{1,0:T(8,128)}, u32[]{:S(2)}) %copy-start.3) | copy-done | bytes 262168
  6.7 0.0 copy-start.4
  6.7 0.9 %copy-done.4 = bf16[512,128]{1,0:T(8,128)(2,1)S(1)} copy-done((bf16[512,128]{1,0:T(8,128)(2,1)S(1)}, bf16[512,128]{1,0:T(8,128)(2,1)}, u32[]{:S(2)}) %copy-start.4) | copy-done | bytes 131096
  7.6 0.0 copy-start.5
  7.6 0.9 %copy-done.5 = bf16[512,128]{1,0:T(8,128)(2,1)S(1)} copy-done((bf16[512,128]{1,0:T(8,128)(2,1)S(1)}, bf16[512,128]{1,0:T(8,128)(2,1)}, u32[]{:S(2)}) %copy-start.5) | copy-done | bytes 131096
  8.5 0.0 copy-start.6
  8.5 0.7 %copy-done.6 = f32[4,512]{1,0:T(4,128)S(1)} copy-done((f32[4,512]{1,0:T(4,128)S(1)}, f32[4,512]{1,0:T(4,128)}, u32[]{:S(2)}) %copy-start.6) | copy-done | bytes 8216
  9.2 0.0 copy-start.7
  9.2 0.7 %copy-done.7 = f32[256]{0:T(256)S(1)} copy-done((f32[256]{0:T(256)S(1)}, f32[256]{0:T(256)}, u32[]{:S(2)}) %copy-start.7) | copy-done | bytes 1048
  9.9 0.0 copy-start.8
  9.9 0.7 %copy-done.8 = f32[12]{0:T(128)S(1)} copy-done((f32[12]{0:T(128)S(1)}, f32[12]{0:T(128)}, u32[]{:S(2)}) %copy-start.8) | copy-done | bytes 72
  10.5 0.0 copy-start.9
  10.5 0.7 %copy-done.9 = s32[4]{0:T(128)S(1)} copy-done((s32[4]{0:T(128)S(1)}, s32[4]{0:T(128)}, u32[]{:S(2)}) %copy-start.9) | copy-done | bytes 40
  11.2 0.0 copy-start.10
  11.2 0.7 %copy-done.10 = s32[4]{0:T(128)S(1)} copy-done((s32[4]{0:T(128)S(1)}, s32[4]{0:T(128)}, u32[]{:S(2)}) %copy-start.10) | copy-done | bytes 40
  11.8 45.1 %shard_map.140 = (f32[2,128]{1,0:T(2,128)S(1)}, bf16[512,128]{1,0:T(8,128)(2,1)S(1)}) custom-call(bf16[512,128]{1,0:T(8,128)(2,1)S(1)} %copy-done.4, bf16[512,128]{1,0:T(8,128)(2,1)S(1)} %copy-done.5, bf16[4,2,256,512]{3,2,1,0:T(8,128)(2,1)S(1)} %copy-done, f32[4,512]{1,0:T(4,128)S(1)} %copy-done.6, bf16[3,256,256]{2,1,0:T(8,128)(2,1)S(1)} %copy-done.2, ...), custom_call_target="tpu_custom_call" | custom-call | flops 1610612736 | bytes 4194304 | tf_op jit(solution)/shard_map/pallas_call | solution.py:283
  57.0 0.6 %slice_reduce_fusion = f32[2]{0:T(128)} fusion(f32[2,128]{1,0:T(2,128)S(1)} %get-tuple-element.4), kind=kLoop, calls=%fused_computation | loop fusion | bytes 16 | tf_op jit(solution)/shard_map/slice | solution.py:318
  57.6 0.7 %copy.19 = bf16[512,128]{1,0:T(8,128)(2,1)} copy(bf16[512,128]{1,0:T(8,128)(2,1)S(1)} %get-tuple-element.9) | data formatting | bytes 262144
Async XLA Ops:
  2.1 1.6 %copy-start = (bf16[4,2,256,512]{3,2,1,0:T(8,128)(2,1)S(1)}, bf16[4,2,256,512]{3,2,1,0:T(8,128)(2,1)}, u32[]{:S(2)}) copy-start(bf16[4,2,256,512]{3,2,1,0:T(8,128)(2,1)} %tap.1) | copy-start | bytes 6291460
  3.7 1.0 %copy-start.1 = (bf16[4,256,256]{2,1,0:T(8,128)(2,1)S(1)}, bf16[4,256,256]{2,1,0:T(8,128)(2,1)}, u32[]{:S(2)}) copy-start(bf16[4,256,256]{2,1,0:T(8,128)(2,1)} %skw.1) | copy-start | bytes 1572868
  4.7 1.0 %copy-start.2 = (bf16[3,256,256]{2,1,0:T(8,128)(2,1)S(1)}, bf16[3,256,256]{2,1,0:T(8,128)(2,1)}, u32[]{:S(2)}) copy-start(bf16[3,256,256]{2,1,0:T(8,128)(2,1)} %res.1) | copy-start | bytes 1179652
  5.7 0.9 %copy-start.3 = (f32[256,256]{1,0:T(8,128)S(1)}, f32[256,256]{1,0:T(8,128)}, u32[]{:S(2)}) copy-start(f32[256,256]{1,0:T(8,128)} %w1.1) | copy-start | bytes 786436
  6.7 0.9 %copy-start.4 = (bf16[512,128]{1,0:T(8,128)(2,1)S(1)}, bf16[512,128]{1,0:T(8,128)(2,1)}, u32[]{:S(2)}) copy-start(bf16[512,128]{1,0:T(8,128)(2,1)} %signal.1) | copy-start | bytes 393220
  7.6 0.9 %copy-start.5 = (bf16[512,128]{1,0:T(8,128)(2,1)S(1)}, bf16[512,128]{1,0:T(8,128)(2,1)}, u32[]{:S(2)}) copy-start(bf16[512,128]{1,0:T(8,128)(2,1)} %skip_in.1) | copy-start | bytes 393220
  8.5 0.7 %copy-start.6 = (f32[4,512]{1,0:T(4,128)S(1)}, f32[4,512]{1,0:T(4,128)}, u32[]{:S(2)}) copy-start(f32[4,512]{1,0:T(4,128)} %bias.1) | copy-start | bytes 24580
  9.2 0.7 %copy-start.7 = (f32[256]{0:T(256)S(1)}, f32[256]{0:T(256)}, u32[]{:S(2)}) copy-start(f32[256]{0:T(256)} %param.20) | copy-start | bytes 3076
  9.9 0.7 %copy-start.8 = (f32[12]{0:T(128)S(1)}, f32[12]{0:T(128)}, u32[]{:S(2)}) copy-start(f32[12]{0:T(128)} %param.22) | copy-start | bytes 148
  10.5 0.7 %copy-start.9 = (s32[4]{0:T(128)S(1)}, s32[4]{0:T(128)}, u32[]{:S(2)}) copy-start(s32[4]{0:T(128)} %bins.1) | copy-start | bytes 52
  11.2 0.7 %copy-start.10 = (s32[4]{0:T(128)S(1)}, s32[4]{0:T(128)}, u32[]{:S(2)}) copy-start(s32[4]{0:T(128)} %flags.1) | copy-start | bytes 52

commit v2 on v1

--- a/solution.py
+++ b/solution.py
@@ -27,20 +27,29 @@
     return 0.5 * jnp.tanh(0.5 * v) + 0.5
 
 
-def head(pooled, bin_at, flag, w1, b1, w2, b2):
-    best = lax.Precision.HIGHEST
-    pre = jnp.dot(pooled, w1, precision=best, preferred_element_type=F32) + b1
-    sig = jax.nn.sigmoid(pre)
+def split3(v):
+    high = v.astype(BF16)
+    rest = v - high.astype(F32)
+    mid = rest.astype(BF16)
+    return high, mid, (rest - mid.astype(F32)).astype(BF16)
+
+
+def row_product(row, parts, product):
+    high, mid, low = (v.astype(F32) for v in split3(row))
+    at = lax.broadcasted_iota(jnp.int32, (8, row.shape[1]), 0)
+    stack = jnp.where(at == 0, high, jnp.where(at == 1, mid, jnp.where(at == 2, low, 0.0))).astype(BF16)
+    total = product(stack, parts[2]) + product(stack, parts[1]) + product(stack, parts[0])
+    return jnp.sum(total, axis=0, keepdims=True)
+
+
+def head(pooled, bin_at, flag, w1_parts, b1, w2, b2):
+    pre = row_product(pooled, w1_parts, mm) + b1
+    sig = sigmoid(pre)
     hidden = pre * sig
-    mixes = w2.shape[1] // 3
-    parts = [w2[:, i * mixes : (i + 1) * mixes] for i in range(3)]
-    p_l, p_s, p_k = (
-        jnp.dot(hidden, parts[i], precision=best, preferred_element_type=F32) + b2[:, i * mixes : (i + 1) * mixes]
-        for i in range(3)
-    )
+    p_l, p_s, p_k = (jnp.sum(w2[i] * hidden, axis=1, keepdims=True) + b2[i] for i in range(3))
     tan_l, log_scale, tan_k = jnp.tanh(p_l), jnp.tanh(p_s), jnp.tanh(p_k)
     logits, log_shape = 4.0 * tan_l, 0.5 * tan_k
-    log_pi = logits - jnp.log(jnp.sum(jnp.exp(logits), axis=1, keepdims=True))
+    log_pi = logits - jnp.log(jnp.sum(jnp.exp(logits), axis=0, keepdims=True))
     shape_value = jnp.exp(log_shape)
     log_time = jnp.log(jnp.full(p_l.shape, (bin_at.astype(F32) + 1.0) / 8.0, F32))
     seen = jnp.full(p_l.shape, flag, jnp.int32) == 1
@@ -49,28 +58,45 @@
     power = jnp.exp(shape_value * ratio)
     density = log_shape - log_scale + (shape_value - 1.0) * ratio - power
     terms = jnp.exp(log_pi + jnp.where(seen, density, -power))
-    total = jnp.sum(terms, axis=1, keepdims=True)
+    total = jnp.sum(terms, axis=0, keepdims=True)
     nll = -jnp.log(total)
     share = terms / total
     d_l = (jnp.exp(log_pi) - share) * 4.0 * (1.0 - tan_l * tan_l)
     d_s = -share * shape_value * (power - seen_one) * (1.0 - log_scale * log_scale)
     d_k = -share * (seen_one + shape_value * ratio * (seen_one - power)) * 0.5 * (1.0 - tan_k * tan_k)
-    d_hidden = mm_t(d_l, parts[0], best) + mm_t(d_s, parts[1], best) + mm_t(d_k, parts[2], best)
+    d_hidden = jnp.sum(d_l * w2[0] + d_s * w2[1] + d_k * w2[2], axis=0, keepdims=True)
     d_pre = d_hidden * sig * (1.0 + pre * (1.0 - sig))
-    return nll, mm_t(d_pre, w1, best)
+    return nll, row_product(d_pre, w1_parts, mm_t)
 
 
 def kernel(
     n, layers, windows,
-    signal, skip_in, tap, bias, res, skw, w1, b1, w2, b2, bins, flags, limit,
+    signal, skip_in, tap_far, bias, res_far, skw_far, w1_far, b1, w2, b2, bins, flags, limit,
     nll_ref, out_ref,
-    xin, skin, old0, xs, olds, tan_f, sig_a, skips, bsend, brecv, b0send, b0recv, a_own, a_send, a_recv, send_sem, recv_sem,
+    xin, skin, old0, xs, olds, tan_f, sig_a, skips, bsend, brecv, b0send, b0recv, a_own, a_send, a_recv, tap, res, skw, w1, w1_split, load_sem, send_sem, recv_sem,
 ):
     me, c = lax.axis_index("tm"), lax.axis_index("chan")
     other = 1 - c
     half = windows * WLEN
     part = signal.shape[1]
     shifts = [n // 16 * 2**k for k in range(layers)]
+
+    load_at = 0
+
+    def load(src, dst):
+        nonlocal load_at
+        this = pltpu.make_async_copy(src, dst, load_sem.at[load_at])
+        this.start()
+        load_at += 1
+        return this
+
+    mine = pl.ds(pl.multiple_of(c * half, half), half)
+    load_x = load(signal.at[mine, :], xin.at[c])
+    load_tap = [load(tap_far.at[0], tap.at[0])]
+    load_res, load_skw = load(res_far, res), load(skw_far, skw)
+    load_skip = load(skip_in.at[mine, :], skin.at[c])
+    load_tap += [load(tap_far.at[k], tap.at[k]) for k in range(1, layers)]
+    load_w1 = load(w1_far, w1)
 
     barrier = pltpu.get_barrier_semaphore()
     expected = jnp.int32(1)
@@ -126,17 +152,16 @@
     def other_rows(j):
         return pl.ds(pl.multiple_of(other * half + j * WLEN, WLEN), WLEN)
 
+    def spot(j):
+        return pl.ds(j * WLEN, WLEN)
+
     chunks = range(windows)
     for j in chunks:
-        send(None, signal.at[other_rows(j), :], xin.at[c, j], X_PART, j, me, other)
+        send(None, signal.at[other_rows(j), :], xin.at[c, spot(j), :], X_PART, j, me, other)
         send(later(0), signal.at[own_rows(j), :], old0.at[c, j], OLD_SAME, j, me + shifts[0], c)
         send(later(0), signal.at[other_rows(j), :], old0.at[c, j], OLD_CROSS, j, me + shifts[0], other)
     for j in chunks:
-        send(None, skip_in.at[other_rows(j), :], skin.at[c, j], SKIP_PART, j, me, other)
-
-    for j in chunks:
-        xin[c, j] = signal[own_rows(j), :]
-        skin[c, j] = skip_in[own_rows(j), :]
+        send(None, skip_in.at[other_rows(j), :], skin.at[c, spot(j), :], SKIP_PART, j, me, other)
 
     @pl.when(me < shifts[0])
     def _():
@@ -158,9 +183,11 @@
 
     width = part * 2
     fresh = {}
+    load_x.wait()
+    load_tap[0].wait()
     for j in chunks:
-        await_in(None, xin.at[other, j], X_PART, j)
-        x = jnp.concatenate([xin[0, j], xin[1, j]], axis=1)
+        await_in(None, xin.at[other, spot(j), :], X_PART, j)
+        x = jnp.concatenate([xin[0, spot(j), :], xin[1, spot(j), :]], axis=1)
         fresh[j] = (x, mm(x, tap[0, 1]) + bias[0:1, :])
 
     def forward(k, j):
@@ -182,17 +209,33 @@
         tan_f[k, j] = fil
         sig_a[k, j] = gate
         if k == 0:
-            await_in(None, skin.at[other, j], SKIP_PART, j)
-            base = jnp.concatenate([skin[0, j], skin[1, j]], axis=1).astype(F32)
+            await_in(None, skin.at[other, spot(j), :], SKIP_PART, j)
+            base = jnp.concatenate([skin[0, spot(j), :], skin[1, spot(j), :]], axis=1).astype(F32)
         else:
             base = skips[j]
         skips[j] = base + mm(z, skw[k])
         if k < layers - 1:
             fresh[j] = (x, mm(x, tap[k + 1, 1]) + bias[k + 1 : k + 2, :])
 
+    load_res.wait()
+    load_skw.wait()
+    load_skip.wait()
     for k in range(layers):
+        if k + 1 < layers:
+            load_tap[k + 1].wait()
         for j in chunks:
             forward(k, j)
+        if k == 0:
+            load_w1.wait()
+            for i, piece in enumerate(split3(w1[...])):
+                w1_split[i] = piece
+    mixes = w2.shape[0] // 3
+    w2_parts = [w2[i * mixes : (i + 1) * mixes, :] for i in range(3)]
+    lane = lax.broadcasted_iota(jnp.int32, (mixes, 3 * mixes), 1)
+    row = lax.broadcasted_iota(jnp.int32, (mixes, 3 * mixes), 0)
+    b2_parts = [
+        jnp.sum(jnp.where(lane == row + i * mixes, b2[...], 0.0), axis=1, keepdims=True) for i in range(3)
+    ]
 
     grads = {}
     own_terms = {}
@@ -208,10 +251,10 @@
         pooled = jnp.sum(s * sig * keep, axis=0, keepdims=True) / jnp.maximum(count, 1.0)
         at = c * windows + j
         nll, grad = head(
-            jnp.broadcast_to(pooled, (8, width)), bins[at], flags[at], w1[...], b1[...], w2[...], b2[...]
+            pooled, bins[at], flags[at], [w1_split[i] for i in range(3)], b1[...], w2_parts, b2_parts
         )
-        nll_ref[j : j + 1, :] = jnp.broadcast_to(nll[0:1, :], (1, nll_ref.shape[1]))
-        grads[j] = (grad[0:1, :] * keep * (sig * (1.0 + s * (1.0 - sig)))).astype(BF16)
+        nll_ref[j : j + 1, :] = jnp.broadcast_to(nll, (1, nll_ref.shape[1]))
+        grads[j] = (grad * keep * (sig * (1.0 + s * (1.0 - sig)))).astype(BF16)
 
     def backward(k, j):
         if k == layers - 1:
@@ -278,6 +321,7 @@
     windows = rows // WLEN // 2
     width = 2 * part
     vmem = pl.BlockSpec(memory_space=pltpu.VMEM)
+    far = pl.BlockSpec(memory_space=pltpu.HBM)
     smem = pl.BlockSpec(memory_space=pltpu.SMEM)
     flops = 2 * windows * WLEN * width * width * (6 * layers + 6 * layers)
     nll, grad = pl.pallas_call(
@@ -286,11 +330,11 @@
             jax.ShapeDtypeStruct((windows, 128), F32),
             jax.ShapeDtypeStruct((rows, part), BF16),
         ),
-        in_specs=[vmem] * 10 + [smem] * 3,
+        in_specs=[far, far, far, vmem, far, far, far, vmem, vmem, vmem, smem, smem, smem],
         out_specs=(vmem, vmem),
         scratch_shapes=[
-            pltpu.VMEM((2, windows, WLEN, part), BF16),
-            pltpu.VMEM((2, windows, WLEN, part), BF16),
+            pltpu.VMEM((2, windows * WLEN, part), BF16),
+            pltpu.VMEM((2, windows * WLEN, part), BF16),
             pltpu.VMEM((2, windows, WLEN, part), BF16),
             pltpu.VMEM((layers - 1, windows, WLEN, width), BF16),
             pltpu.VMEM((layers - 1, windows, WLEN, width), BF16),
@@ -304,16 +348,22 @@
             pltpu.VMEM((2, windows, WLEN, part), F32),
             pltpu.VMEM((2, windows, WLEN, part), BF16),
             pltpu.VMEM((windows, WLEN, part), BF16),
+            pltpu.VMEM(tap_weight.shape, BF16),
+            pltpu.VMEM(res_weight.shape, BF16),
+            pltpu.VMEM(skip_weight.shape, BF16),
+            pltpu.VMEM(head_w1.shape, F32),
+            pltpu.VMEM((3, *head_w1.shape), BF16),
+            pltpu.SemaphoreType.DMA((layers + 5,)),
             pltpu.SemaphoreType.DMA((ITEMS, windows)),
             pltpu.SemaphoreType.DMA((ITEMS, windows)),
         ],
         compiler_params=pltpu.CompilerParams(
-            collective_id=0, has_side_effects=True, vmem_limit_bytes=40 * 1024 * 1024
+            collective_id=0, has_side_effects=True, vmem_limit_bytes=60 * 1024 * 1024
         ),
         cost_estimate=pl.CostEstimate(flops=flops, bytes_accessed=4 * 1024 * 1024, transcendentals=0),
     )(
         signal, skip_in, tap_weight, tap_bias, res_weight, skip_weight,
-        head_w1, head_b1[None, :], head_w2, head_second_bias[None, :], event_bin, observed, valid_len,
+        head_w1, head_b1[None, :], head_w2.T, head_second_bias[None, :], event_bin, observed, valid_len,
     )
     return nll[:, 0], grad
 

time: 58.7 us -> 48.5 us (0.83)
  local copies, waits for them, and re-layouts: 11.8 us -> 2.85 us
  Pallas kernels: 45.1 us -> 44.2 us
    unnamed x24 -> x1, local copies, waits for them, and re-layouts: 11.2 us -> 1.57 us
    pallas_call x1, Pallas kernels: 45.1 us -> 44.2 us  [local(): pl.pallas_call(functools.partial(kernel, n, layers, windows), out_shape=(...]
    slice x1, local copies, waits for them, and re-layouts: 0.63 us -> 1.29 us  [local(): return (nll[:, 0], grad)]
where the time goes in v2:
time: 48.5 us; the launch traced here: 48.3 us
  Pallas kernels  44.2 us (91%)
  local copies, waits for them, and re-layouts  2.85 us (6%)
  between operations  1.29 us (3%)
    pallas_call x1, Pallas kernels, local(): pl.pallas_call(functools.partial(kernel, n, layers, windows), out_shape=(...  44.2 us
    unnamed x1, local copies, waits for them, and re-layouts  1.57 us
    slice x1, local copies, waits for them, and re-layouts, local(): return (nll[:, 0], grad)  1.29 us

profile of v2, /device:TPU:0, one launch (start us, length us, event | category | flops | bytes accessed | tf_op | source)
XLA Modules:
  0.0 48.3 jit_solution(8831521147329514640)
XLA Ops:
  1.3 44.2 %shard_map.140 = (f32[2,128]{1,0:T(2,128)}, bf16[512,128]{1,0:T(8,128)(2,1)}) custom-call(bf16[512,128]{1,0:T(8,128)(2,1)} %signal.1, bf16[512,128]{1,0:T(8,128)(2,1)} %skip_in.1, bf16[4,2,256,512]{3,2,1,0:T(8,128)(2,1)} %tap_far.1, f32[4,512]{1,0:T(4,128)} %bias.1, bf16[3,256,256]{2,1,0:T(8,128)(2,1)} %res_far.1, bf16[4,256,256]{2,1,0:T(8,128)(2,1)} %skw_far.1, ...), custom_call_target="tpu_custom_call" | custom-call | flops 1610612736 | bytes 4194304 | tf_op jit(solution)/shard_map/pallas_call | solution.py:327
  45.5 1.3 %slice_reduce_fusion = f32[2]{0:T(128)} fusion(f32[2,128]{1,0:T(2,128)} %get-tuple-element.4), kind=kLoop, calls=%fused_computation | loop fusion | bytes 16 | tf_op jit(solution)/shard_map/slice | solution.py:368
  46.8 1.6 %copy.17 = bf16[512,128]{1,0:T(8,128)(2,1)} copy(bf16[512,128]{1,0:T(8,128)(2,1)} %get-tuple-element.9) | data formatting | bytes 262144
